TPU v7x, 512 devices: a whole 4x4x16 slice. The times are simulated.
512 devices in a mesh: fsdp: 128 (over y, z, core), tp: 4 (over x).
Axes of the slice: x: 4, y: 4, z: 16, core: 2. Of those that a mesh axis runs over, the one named last changes fastest.
Arguments:
- grads: bfloat16 [16, 512, 16, 512], P(None, 'fsdp', None, 'tp'), may hold values from -1.5 to 1.5
- second_moment: bfloat16 [16, 512, 16, 512], P(None, 'fsdp', None, 'tp'), may hold values from 0.0009994507 to 0.099609375
- owner: int32 [16, 16], replicated, may hold values from 0 to 127, as said below
- left_factor: bfloat16 [640, 512, 512], P('fsdp', 'tp'), may hold values from -1 to 11
- right_factor: bfloat16 [640, 512, 512], P('fsdp', 'tp'), may hold values from -1 to 11
- left_root: bfloat16 [640, 512, 512], P('fsdp', 'tp'), may hold values from -0.2 to 1.2
- right_root: bfloat16 [640, 512, 512], P('fsdp', None, 'tp'), may hold values from -0.2 to 1.2
Outputs:
- update: bfloat16 [16, 512, 16, 512], P(None, 'fsdp', None, 'tp')
- moment_new: bfloat16 [16, 512, 16, 512], P(None, 'fsdp', None, 'tp')
- left_new: bfloat16 [640, 512, 512], P('fsdp', 'tp')
- right_new: bfloat16 [640, 512, 512], P('fsdp', 'tp')
Inputs may be any that keep to these rules, and one draw needn't show every extreme that they name: No owner holds more than 5 blocks and some owner holds exactly 5; no owner holds more than 2 blocks of one block row and some owner holds exactly 2; the 4 consecutive owners starting at some owner hold none.
All inputs are finite; a program needn't handle non-finite values.
Results may differ from a plain program's by a relative error of at most 0.0057.
Values may be sent and summed in bfloat16 or wider, within the bound.
A program may use at most 64 MiB of HBM per device.

v0:
```python
import jax
import jax.numpy as jnp
from jax import lax
from jax.sharding import PartitionSpec as P

beta_factor = 0.9
beta_moment = 0.95
eps_moment = 1e-08
eps_norm = 1e-06


def earlier_same(values):
    length = values.shape[-1]
    order = jnp.arange(length)
    same = values[..., :, None] == values[..., None, :]
    before = order[None, :] < order[:, None]
    return jnp.sum((same & before).astype(jnp.int32), axis=-1)


def per_device(grads, second_moment, owner, left_factor, right_factor, left_root, right_root):
    block_rows, strip_rows, col_blocks, quarter = grads.shape
    owner_count = lax.axis_size("fsdp")
    column_count = lax.axis_size("tp")
    block_size = quarter * column_count
    slot_count = left_factor.shape[0]
    column_part = lax.axis_index("tp")
    slot_rank = earlier_same(owner.reshape(-1)).reshape(owner.shape)
    owner_hit = owner[None] == jnp.arange(owner_count)[:, None, None]
    rank_hit = slot_rank[None] == jnp.arange(slot_count)[:, None, None]
    select = (owner_hit[:, None] & rank_hit[None]).astype(jnp.bfloat16)
    select = select.reshape(owner_count * slot_count, block_rows, col_blocks)
    grad_float = grads.astype(jnp.float32)
    moment = (
        beta_moment * second_moment.astype(jnp.float32)
        + (1.0 - beta_moment) * grad_float * grad_float
    )
    adam = grad_float / (jnp.sqrt(moment) + eps_moment)
    adam_part = jnp.sum(adam * adam, axis=(1, 3))
    send_pieces = jnp.einsum("qij,irjc->qrc", select, grads, preferred_element_type=jnp.float32)
    send_pieces = send_pieces.astype(jnp.bfloat16).reshape(
        owner_count, slot_count, strip_rows, quarter
    )
    received = lax.all_to_all(send_pieces, "fsdp", split_axis=0, concat_axis=2, tiled=True)
    local_cols = received.reshape(slot_count, block_size, quarter)
    full_block = lax.all_gather(local_cols, "tp", axis=2, tiled=True)
    own_rows = lax.dynamic_slice_in_dim(full_block, column_part * quarter, quarter, 1)
    gram_left = jnp.einsum("sic,sjc->sij", own_rows, full_block, preferred_element_type=jnp.float32)
    left_new = (
        beta_factor * left_factor.astype(jnp.float32) + (1.0 - beta_factor) * gram_left
    ).astype(jnp.bfloat16)
    gram_right = jnp.einsum(
        "sri,srj->sij", local_cols, full_block, preferred_element_type=jnp.float32
    )
    right_new = (
        beta_factor * right_factor.astype(jnp.float32) + (1.0 - beta_factor) * gram_right
    ).astype(jnp.bfloat16)
    rotated = jnp.einsum(
        "sik,skj->sij", left_root, full_block, preferred_element_type=jnp.float32
    ).astype(jnp.bfloat16)
    rotated_whole = lax.all_gather(rotated, "tp", axis=1, tiled=True)
    precond = jnp.einsum(
        "sik,skj->sij", rotated_whole, right_root, preferred_element_type=jnp.float32
    ).astype(jnp.bfloat16)
    sectioned = precond.reshape(1, slot_count, block_size, quarter)
    returned = lax.all_to_all(sectioned, "fsdp", split_axis=2, concat_axis=0, tiled=True)
    returned = returned.reshape(owner_count * slot_count, strip_rows, quarter)
    placed = jnp.einsum("qij,qrc->irjc", select, returned, preferred_element_type=jnp.float32)
    placed = placed.astype(jnp.bfloat16)
    placed_float = placed.astype(jnp.float32)
    pre_part = jnp.sum(placed_float * placed_float, axis=(1, 3))
    adam_sums, pre_sums = lax.psum((adam_part, pre_part), ("fsdp", "tp"))
    block_scale = jnp.sqrt(adam_sums) / (jnp.sqrt(pre_sums) + eps_norm)
    update = (placed_float * block_scale[:, None, :, None]).astype(jnp.bfloat16)
    return (update, moment.astype(jnp.bfloat16), left_new, right_new)


def solution(mesh):
    in_specs = (
        P(None, "fsdp", None, "tp"),
        P(None, "fsdp", None, "tp"),
        P(),
        P("fsdp", "tp", None),
        P("fsdp", "tp", None),
        P("fsdp", "tp", None),
        P("fsdp", None, "tp"),
    )
    out_specs = (
        P(None, "fsdp", None, "tp"),
        P(None, "fsdp", None, "tp"),
        P("fsdp", "tp", None),
        P("fsdp", "tp", None),
    )
    return jax.shard_map(
        per_device, mesh=mesh, in_specs=in_specs, out_specs=out_specs, check_vma=False
    )
```

profile of v0, /device:TPU:1, one launch (start us, length us, event | category | flops | bytes accessed | tf_op | source)
XLA Modules:
  0.0 343.5 jit_solution(9382370383889696945)
XLA Ops:
  7.2 0.0 copy-start
  7.2 0.0 all-gather.3.cloned.1.call-start
  7.2 0.8 eq.54
  8.1 0.8 iota_compare_fusion
  8.9 0.2 convert_reduce_fusion
  9.1 0.1 eq.58
  9.2 0.0 copy-start.4
  9.2 0.6 broadcast_and_fusion
  9.8 2.2 copy.53
  12.1 0.4 fusion.4
  12.5 0.5 copy.55
  13.0 58.6 %all_to_all.30 = bf16[128,5,4,128]{3,2,1,0:T(4,128)(2,1)S(1)} all-to-all(bf16[128,5,4,128]{3,2,1,0:T(4,128)(2,1)S(1)} %bitcast.47), channel_id=1, replica_groups=mesh['fsdp'=128,'tp'=4] {'fsdp'}, dimensions={0} | all-to-all | bytes 1310720 | tf_op jit(solution)/shard_map/all_to_all | solution.py:43
  71.6 0.2 copy.56
  71.9 1.1 copy.57
  73.0 0.0 all-gather.3.cloned.1.call-update
  73.0 0.0 all-gather.5.cloned.1.call-start
  73.0 35.4 %all-gather.3.cloned.1.call-done = bf16[5,512,512]{1,2,0:T(8,128)(2,1)} async-done(((bf16[5,512,128]{1,2,0:T(8,128)(2,1)}), bf16[5,512,512]{1,2,0:T(8,128)(2,1)}) %all-gather.3.cloned.1.call-update) | async-done | bytes 2621456 | tf_op jit(solution)/shard_map/all_gather | solution.py:45
  108.5 3.4 fusion.5
  111.9 0.0 all-gather.5.cloned.1.call-update
  111.9 46.0 %all-gather.5.cloned.1.call-done = bf16[5,512,512]{1,2,0:T(8,128)(2,1)} async-done(((bf16[5,128,512]{1,2,0:T(8,128)(2,1)}), bf16[5,512,512]{1,2,0:T(8,128)(2,1)}) %all-gather.5.cloned.1.call-update) | async-done | bytes 2621456 | tf_op jit(solution)/shard_map/all_gather | solution.py:60
  157.9 2.8 fusion.6
  160.7 1.5 copy.59
  162.1 17.7 %all-to-all-start.1 = ((bf16[1,5,512,128]{3,1,0,2:T(8,128)(2,1)}), bf16[1,5,512,128]{3,1,0,2:T(8,128)(2,1)S(1)}, u32[]{:S(2)}, u32[]{:S(2)}) async-start(bf16[1,5,512,128]{3,1,0,2:T(8,128)(2,1)} %copy.59), calls=%async_computation.1 | async-start | bytes 2097152 | tf_op jit(solution)/shard_map/all_to_all | solution.py:65
  179.8 1.0 fusion.14
  180.8 3.7 %fusion.2 = bf16[5,128,512]{2,1,0:T(8,128)(2,1)} fusion(bf16[5,512,512]{1,2,0:T(8,128)(2,1)} %all-gather.3.cloned.1.call-done, bf16[5,128,512]{2,1,0:T(8,128)(2,1)} %param.10, s32[]{:T(128)S(6)} %select_n.3), kind=kOutput, calls=%fused_computation.6 | convolution fusion | flops 337182720 | bytes 4587524 | tf_op jit(solution)/shard_map/sic,sjc->sij/dot_general | solution.py:47
  184.5 1.9 fusion.3
  186.4 47.8 %all-to-all-done.1 = bf16[1,5,512,128]{3,1,0,2:T(8,128)(2,1)S(1)} async-done(((bf16[1,5,512,128]{3,1,0,2:T(8,128)(2,1)}), bf16[1,5,512,128]{3,1,0,2:T(8,128)(2,1)S(1)}, u32[]{:S(2)}, u32[]{:S(2)}) %all-to-all-start.1) | async-done | bytes 655392 | tf_op jit(solution)/shard_map/all_to_all | solution.py:65
  234.1 0.3 copy.60
  234.4 0.5 multiply_reduce_fusion
  234.9 100.9 %all-reduce = (f32[16,16]{1,0:T(8,128)S(1)}, f32[16,16]{1,0:T(8,128)S(1)}) all-reduce(f32[16,16]{1,0:T(8,128)S(1)} %get-tuple-element.28, f32[16,16]{1,0:T(8,128)S(1)} %get-tuple-element.27), channel_id=1, replica_groups=mesh['fsdp'=128,'tp'=4] {'fsdp','tp'}, use_global_device_ids=true, to_apply=%region_4.0 | all-reduce | flops 512 | bytes 4096 | tf_op jit(solution)/shard_map/psum | solution.py:71
  335.8 0.1 fusion.16
  336.0 0.7 copy.67
  (12 shorter events, 0.0 us)
Async XLA Ops:
  7.2 101.3 %copy-start = (bf16[5,128,512]{2,1,0:T(8,128)(2,1)S(1)}, bf16[5,128,512]{2,1,0:T(8,128)(2,1)}, u32[]{:S(2)}) copy-start(bf16[5,128,512]{2,1,0:T(8,128)(2,1)} %param.12) | copy-start | bytes 1966084
  7.2 101.3 %all-gather.3.cloned.1.call-start = ((), (), s32[]{:S(2)}) async-start(), calls=%async_computation.2 | async-start | bytes 3276800 | tf_op jit(solution)/shard_map/all_gather | solution.py:45
  9.2 2.9 copy-start.4
  73.0 84.9 %copy-start.3 = (bf16[5,512,128]{2,1,0:T(8,128)(2,1)S(1)}, bf16[5,512,128]{2,1,0:T(8,128)(2,1)}, u32[]{:S(2)}) copy-start(bf16[5,512,128]{2,1,0:T(8,128)(2,1)} %param.13) | copy-start | bytes 1966084
  73.0 84.9 %all-gather.5.cloned.1.call-start = ((), (), s32[]{:S(2)}) async-start(), calls=%async_computation.3 | async-start | bytes 3276800 | tf_op jit(solution)/shard_map/all_gather | solution.py:60
  162.1 17.7 %copy-start.5 = (bf16[16,4,16,128]{3,2,1,0:T(8,128)(2,1)S(1)}, bf16[16,4,16,128]{3,2,1,0:T(8,128)(2,1)}, u32[]{:S(2)}) copy-start(bf16[16,4,16,128]{3,2,1,0:T(8,128)(2,1)} %param.8) | copy-start | bytes 786436
  162.1 72.0 %all-to-all-start.1 = ((bf16[1,5,512,128]{3,1,0,2:T(8,128)(2,1)}), bf16[1,5,512,128]{3,1,0,2:T(8,128)(2,1)S(1)}, u32[]{:S(2)}, u32[]{:S(2)}) async-start(bf16[1,5,512,128]{3,1,0,2:T(8,128)(2,1)} %copy.59), calls=%async_computation.1 | async-start | bytes 2097152 | tf_op jit(solution)/shard_map/all_to_all | solution.py:65
  180.8 3.7 %copy-start.1 = (bf16[5,512,512]{1,2,0:T(8,128)(2,1)S(1)}, bf16[5,512,512]{1,2,0:T(8,128)(2,1)}, u32[]{:S(2)}) copy-start(bf16[5,512,512]{1,2,0:T(8,128)(2,1)} %all-gather.3.cloned.1.call-done) | copy-start | bytes 7864324
  180.8 3.7 %copy-start.2 = (bf16[5,128,512]{2,1,0:T(8,128)(2,1)S(1)}, bf16[5,128,512]{2,1,0:T(8,128)(2,1)}, u32[]{:S(2)}) copy-start(bf16[5,128,512]{2,1,0:T(8,128)(2,1)} %param.11) | copy-start | bytes 1966084
Sparse Core Ops, SparseCore 0:
  73.1 35.3 all-gather.2
  112.0 45.8 all-gather.4
where the time goes:
time: 344 us
  blocking collectives  160 us (47%)
  waiting for transfers between devices  129 us (38%)
  starting transfers between devices  17.7 us (5%)
  between operations  14.2 us (4%)
  matrix products  12.6 us (4%)
  local copies, waits for them, and re-layouts  7.47 us (2%)
    psum x1, blocking collectives, per_device(): adam_sums, pre_sums = lax.psum((adam_part, pre_part), ('fsdp', 'tp'))  101 us
    all_to_all x1, blocking collectives, per_device(): lax.all_to_all(send_pieces, 'fsdp', split_axis=0, concat_axis=2, tiled=True)  58.6 us
    all_to_all x1, waiting for transfers between devices, per_device(): lax.all_to_all(sectioned, 'fsdp', split_axis=2, concat_axis=0, tiled=True)  47.8 us
    all_gather x1, waiting for transfers between devices, per_device(): rotated_whole = lax.all_gather(rotated, 'tp', axis=1, tiled=True)  46 us
    all_gather x1, waiting for transfers between devices, per_device(): full_block = lax.all_gather(local_cols, 'tp', axis=2, tiled=True)  35.4 us
    all_to_all x1, starting transfers between devices, per_device(): lax.all_to_all(sectioned, 'fsdp', split_axis=2, concat_axis=0, tiled=True)  17.7 us
  transfers between devices with their start and end apart: 3, of which 3 were waited for; matrix products, arithmetic and copies ran while one was open for 2% of the time, Pallas kernels for 0%

commit v1 on v0

v1 whole, which is shorter than its diff:
```python
import functools
import types

import jax
import jax.numpy as jnp
from jax import lax
from jax.experimental import pallas as pl
from jax.experimental.pallas import tpu as pltpu
from jax.sharding import PartitionSpec as P

BF, F32, I32 = jnp.bfloat16, jnp.float32, jnp.int32
MESH = pl.DeviceIdType.MESH
CAP = 5
MAIN = 2
REST = CAP - MAIN
LANES = 128


def cfg_of(NY, NZ, NC, NX, R, Q, NBR, NBC, CB, cid):
    c = types.SimpleNamespace(NY=NY, NZ=NZ, NC=NC, NX=NX, R=R, Q=Q, NBR=NBR, NBC=NBC, CB=CB, cid=cid)
    c.NG = NY * NC
    c.NB = NBR * NBC
    c.B = NX * Q
    c.W = R * Q
    assert c.B == NY * NZ * NC * R
    return c


def idiv(x, d):
    if d & (d - 1) == 0:
        return lax.shift_right_logical(x, jnp.int32(d.bit_length() - 1))
    return lax.shift_right_logical(x * jnp.int32(-(-(1 << 16) // d)), jnp.int32(16))


def imod(x, d):
    if d & (d - 1) == 0:
        return x & jnp.int32(d - 1)
    return x - idiv(x, d) * jnp.int32(d)


def iota(shape, dim):
    return lax.broadcasted_iota(I32, shape, dim)


def hot(cond):
    return jnp.where(cond, 1.0, 0.0).astype(BF)


def dot(a, b):
    return jnp.dot(a, b, preferred_element_type=F32)


def scratch_of(c):
    vm = lambda *s: pltpu.VMEM(s, BF)
    vf = lambda *s: pltpu.VMEM(s, F32)
    dma = lambda *s: pltpu.SemaphoreType.DMA(s)
    out = {}
    for name in ("sA", "rA", "sI", "rI"):
        out[name] = vm(c.NZ, MAIN * c.NG, c.W)
    for name in ("sB", "rB", "sJ", "rJ"):
        out[name] = vm(c.NZ, c.R * c.CB, c.Q)
    for name in ("sC", "rC", "sF", "rF"):
        out[name] = vm(c.NG, MAIN, c.NZ, c.W)
    for name in ("sE", "rE", "sH", "rH"):
        out[name] = vm(c.NG, REST, c.NZ, c.W)
    out["gown"] = vm(CAP, c.B, c.Q)
    out["gfull"] = vm(CAP, c.B, c.B)
    out["lfull"] = vm(CAP, c.B, c.B)
    out["rv"] = vm(CAP, c.B, c.Q)
    for name in ("lfv", "rfv", "lnv", "rnv"):
        out[name] = vm(CAP, c.Q, c.B)
    out["pre"] = vf(CAP, c.B, c.Q)
    out["pi"] = vm(c.B, c.B)
    out["pit"] = vm(c.B, c.B)
    out["az"] = vf(c.NZ, 1, LANES)
    out["azr"] = vf(c.NZ, 1, LANES)
    out["ag"] = vf(1, 1, LANES)
    out["agr"] = vf(c.NG, 1, LANES)
    for name in ("ax", "pa", "pb"):
        out[name] = vf(1, 1, LANES)
        out[name + "r"] = vf(c.NX, 1, LANES)
    for name in ("A", "B", "I", "J", "z"):
        out["s_" + name], out["r_" + name] = dma(c.NZ), dma(c.NZ)
    for name in ("C", "E", "F", "H", "g"):
        out["s_" + name], out["r_" + name] = dma(c.NG), dma(c.NG)
    for name in ("x", "pa", "pb"):
        out["s_" + name], out["r_" + name] = dma(c.NX), dma(c.NX)
    for name in ("L1", "L2", "G1", "G2"):
        out["s_" + name], out["r_" + name] = dma(CAP, 2), dma(CAP, 2)
    for name in ("l_lf", "l_rf", "l_rv", "l_lr", "l_ln", "l_rn"):
        out[name] = dma(CAP)
    return out


def kernel(c, names, grads, sm, owner, lf, rf, lr, rr, upd, mom, ln, rn, *scratch):
    w = types.SimpleNamespace(**dict(zip(names, scratch)))
    NZ, NG, NX, NB, R, Q, B, W, CB = c.NZ, c.NG, c.NX, c.NB, c.R, c.Q, c.B, c.W, c.CB
    f = lax.axis_index("fsdp")
    t = lax.axis_index("tp")
    me_c = lax.rem(f, c.NC)
    me_z = lax.rem(lax.div(f, c.NC), NZ)
    me_y = lax.div(f, c.NC * NZ)
    me_g = me_y * c.NC + me_c
    right, left = lax.rem(t + 1, NX), lax.rem(t + NX - 1, NX)

    def at_z(z):
        return {"fsdp": (me_y * NZ + z) * c.NC + me_c, "tp": t}

    def at_g(g):
        return {"fsdp": (lax.div(g, c.NC) * NZ + me_z) * c.NC + lax.rem(g, c.NC), "tp": t}

    def at_x(x):
        return {"fsdp": f, "tp": x}

    def rcopy(src, dst, ssem, rsem, dev):
        return pltpu.make_async_remote_copy(
            src_ref=src, dst_ref=dst, send_sem=ssem, recv_sem=rsem, device_id=dev, device_id_type=MESH
        )

    def loop(lo, hi, body):
        def step(k, carry):
            body(k)
            return carry
        lax.fori_loop(lo, hi, step, 0)

    def each_z(body):
        half = NZ // 2
        body(lax.rem(me_z + half, NZ))
        if half > 1:
            def pair(k):
                d = half - 1 - k
                body(lax.rem(me_z + d, NZ))
                body(lax.rem(me_z + NZ - d, NZ))
            loop(0, half - 1, pair)

    def each_g(body):
        loop(1, NG, lambda k: body(lax.rem(me_g + k, NG)))

    def each_x(body):
        loop(1, NX, lambda k: body(lax.rem(t + k, NX)))

    class Exchange:
        def __init__(self, each, at, me, src, dst, sems):
            self.each, self.at, self.me, self.src, self.dst = each, at, me, src, dst
            self.ss, self.rs = getattr(w, "s_" + sems), getattr(w, "r_" + sems)

        def start(self):
            def go(p):
                rcopy(self.src(p), self.dst.at[self.me], self.ss.at[p], self.rs.at[self.me], self.at(p)).start()
            self.each(go)

        def recv(self):
            def go(p):
                rcopy(self.src(p), self.dst.at[p], self.ss.at[p], self.rs.at[p], self.at(p)).wait_recv()
            self.each(go)

        def sent(self):
            def go(p):
                rcopy(self.src(p), self.dst.at[p], self.ss.at[p], self.rs.at[p], self.at(p)).wait_send()
            self.each(go)

    def one(buf):
        return lambda p: buf.at[0]

    def many(buf):
        return lambda p: buf.at[p]

    xA = Exchange(each_z, at_z, me_z, many(w.sA), w.rA, "A")
    xB = Exchange(each_z, at_z, me_z, many(w.sB), w.rB, "B")
    xI = Exchange(each_z, at_z, me_z, many(w.sI), w.rI, "I")
    xJ = Exchange(each_z, at_z, me_z, many(w.sJ), w.rJ, "J")
    xz = Exchange(each_z, at_z, me_z, many(w.az), w.azr, "z")
    xC = Exchange(each_g, at_g, me_g, many(w.sC), w.rC, "C")
    xE = Exchange(each_g, at_g, me_g, many(w.sE), w.rE, "E")
    xF = Exchange(each_g, at_g, me_g, many(w.sF), w.rF, "F")
    xH = Exchange(each_g, at_g, me_g, many(w.sH), w.rH, "H")
    xg = Exchange(each_g, at_g, me_g, one(w.ag), w.agr, "g")
    xx = Exchange(each_x, at_x, t, one(w.ax), w.axr, "x")
    xpa = Exchange(each_x, at_x, t, one(w.pa), w.par, "pa")
    xpb = Exchange(each_x, at_x, t, one(w.pb), w.pbr, "pb")

    def shard_rows(x):
        return pl.multiple_of(x * Q, Q)

    def l_first(s, d):
        dst = w.lfull.at[s, pl.ds(shard_rows(t), Q), :]
        return rcopy(lr.at[s], dst, w.s_L1.at[s, d], w.r_L1.at[s, d], at_x(right if d == 0 else left))

    def l_pass(s, d):
        x = left if d == 0 else right
        part = w.lfull.at[s, pl.ds(pl.multiple_of(x * Q + d * (Q // 2), Q // 2), Q // 2), :]
        return rcopy(part, part, w.s_L2.at[s, d], w.r_L2.at[s, d], at_x(right if d == 0 else left))

    def g_first(s, d):
        dst = w.gfull.at[s, :, pl.ds(shard_rows(t), Q)]
        return rcopy(w.gown.at[s], dst, w.s_G1.at[s, d], w.r_G1.at[s, d], at_x(right if d == 0 else left))

    def g_pass(s, d):
        x = left if d == 0 else right
        part = w.gfull.at[s, pl.ds(d * (B // 2), B // 2), pl.ds(shard_rows(x), Q)]
        return rcopy(part, part, w.s_G2.at[s, d], w.r_G2.at[s, d], at_x(right if d == 0 else left))

    def pass_on(first, onward, s):
        for d in (0, 1):
            first(s, d).wait_recv()
            onward(s, d).start()

    barrier = pltpu.get_barrier_semaphore()

    def greet(at):
        def go(p):
            pl.semaphore_signal(barrier, inc=1, device_id=at(p), device_id_type=MESH)
        return go
    each_z(greet(at_z))
    each_g(greet(at_g))
    each_x(greet(at_x))

    def local(src, dst, sem):
        return pltpu.make_async_copy(src, dst, sem)

    def l_own(s):
        return local(lr.at[s], w.lfull.at[s, pl.ds(shard_rows(t), Q), :], w.l_lr.at[s])

    def loads(s):
        return (
            local(rr.at[s], w.rv.at[s], w.l_rv.at[s]),
            local(lf.at[s], w.lfv.at[s], w.l_lf.at[s]),
            local(rf.at[s], w.rfv.at[s], w.l_rf.at[s]),
        )

    spread = hot(imod(iota((c.NBC, NB), 1), c.NBC) == iota((c.NBC, NB), 0))
    wide = dot(owner[...].astype(F32).astype(BF), spread)
    own_row = jnp.sum(
        jnp.where(idiv(iota((c.NBR, NB), 1), c.NBC) == iota((c.NBR, NB), 0), wide, 0.0), axis=0, keepdims=True
    )
    i0, i1 = iota((NB, NB), 0), iota((NB, NB), 1)
    own_col = jnp.sum(jnp.where(i0 == i1, own_row, 0.0), axis=1, keepdims=True)
    same = own_row == own_col
    rank_row = jnp.sum(jnp.where(same & (i0 < i1), 1.0, 0.0), axis=0, keepdims=True).astype(I32)
    rank_col = jnp.sum(jnp.where(same & (i1 < i0), 1.0, 0.0), axis=1, keepdims=True).astype(I32)
    own_row, own_col = own_row.astype(I32), own_col.astype(I32)
    key_row, key_col = own_row * 8 + rank_row, own_col * 8 + rank_col
    z_row, z_col = imod(idiv(own_row, c.NC), NZ), imod(idiv(own_col, c.NC), NZ)

    def key_of(z, g, s):
        return ((idiv(g, c.NC) * NZ + z) * c.NC + imod(g, c.NC)) * 8 + s

    def key_main(m):
        return key_of(idiv(m, MAIN * NG), imod(m, NG), imod(idiv(m, NG), MAIN))

    places = NZ * MAIN * NG
    sel_main = hot(key_main(iota((places, 1), 0)) == key_row)
    for r in range(R):
        block = grads[:, r, :, :].reshape(NB, Q)
        w.sA[:, :, r * Q:(r + 1) * Q] = dot(sel_main, block).astype(BF).reshape(NZ, MAIN * NG, Q)

    pl.semaphore_wait(barrier, NZ - 1 + NG - 1 + NX - 1)
    xA.start()
    for s in range(MAIN):
        for d in (0, 1):
            l_first(s, d).start()

    over_row, over_col = rank_row >= MAIN, rank_col >= MAIN
    mates = (z_row == z_col)
    pos_row = jnp.sum(jnp.where(mates & over_col & (i0 < i1), 1.0, 0.0), axis=0, keepdims=True).astype(I32)
    pos_col = jnp.sum(jnp.where(mates & over_row & (i1 < i0), 1.0, 0.0), axis=1, keepdims=True).astype(I32)
    PB = NZ * R * CB
    rest_row = jnp.where(over_row & (pos_row < CB), z_row * CB + pos_row, -1)
    rest_col = jnp.where(over_col & (pos_col < CB), z_col * CB + pos_col, -1)

    def rest_parts(m):
        return idiv(m, R * CB), imod(idiv(m, CB), R), imod(m, CB)

    mz, mr, mb = rest_parts(iota((PB, 1), 0))
    lz, lrr, lb = rest_parts(iota((1, PB), 1))
    m_rest, l_rest = mz * CB + mb, lz * CB + lb
    total = jnp.zeros((PB, Q), F32)
    for r in range(R):
        sel = hot(jnp.where(mr == r, m_rest, -2) == rest_row)
        total += dot(sel, grads[:, r, :, :].reshape(NB, Q))
    w.sB[...] = total.astype(BF).reshape(NZ, R * CB, Q)
    xB.start()
    w.rA[pl.ds(me_z, 1)] = w.sA[pl.ds(me_z, 1)]
    w.rB[pl.ds(me_z, 1)] = w.sB[pl.ds(me_z, 1)]
    for s in range(MAIN, CAP):
        for d in (0, 1):
            l_first(s, d).start()
    for s in range(CAP):
        l_own(s).start()
        for copy in loads(s):
            copy.start()

    adam_col = jnp.zeros((NB, 1), F32)
    for r in range(R):
        g = grads[:, r, :, :].astype(F32)
        moment = 0.95 * sm[:, r, :, :].astype(F32) + 0.05 * g * g
        mom[:, r, :, :] = moment.astype(BF)
        adam = g / (jnp.sqrt(moment) + 1e-08)
        adam_col += jnp.sum((adam * adam).reshape(NB, Q), axis=1, keepdims=True)
    lane = iota((1, LANES), 1)
    lane_key = jnp.where(lane < NG * 8, key_of(jnp.zeros_like(lane), idiv(lane, 8), imod(lane, 8)), -1)

    def sums_for(z):
        hit = (key_col - z * (c.NC * 8)) == lane_key
        w.az[pl.ds(z, 1)] = jnp.sum(jnp.where(hit, adam_col, 0.0), axis=0, keepdims=True)[None]
    loop(0, NZ, sums_for)
    xz.start()
    w.azr[pl.ds(me_z, 1)] = w.az[pl.ds(me_z, 1)]

    def natural(m):
        r, g, z = idiv(m, NG * NZ), imod(idiv(m, NZ), NG), imod(m, NZ)
        return ((idiv(g, c.NC) * NZ + z) * c.NC + imod(g, c.NC)) * R + r
    w.pi[...] = hot(iota((B, B), 0) == natural(iota((1, B), 1)))
    w.pit[...] = hot(natural(iota((B, 1), 0)) == iota((B, B), 1))

    def turned(m):
        return (imod(m, NZ) * MAIN + imod(idiv(m, NZ), MAIN)) * NG + idiv(m, NZ * MAIN)
    to_gsz = hot(turned(iota((places, 1), 0)) == iota((places, places), 1))
    to_zsg = hot(iota((places, places), 0) == turned(iota((1, places), 1)))

    held_row = jnp.sum(
        jnp.where(rest_col == me_z * CB + lb, key_col + 1, 0), axis=0, keepdims=True
    ) - 1
    held_col = jnp.sum(
        jnp.where(me_z * CB + mb == rest_row, key_row + 1, 0), axis=1, keepdims=True
    ) - 1

    def rest_slots(m):
        return idiv(m, REST * NZ), imod(idiv(m, NZ), REST) + MAIN, imod(m, NZ)
    PS = NG * REST * NZ
    ag_, as_, az_ = rest_slots(iota((PS, 1), 0))
    slot_col = key_of(me_z, ag_, as_)
    bg_, bs_, bz_ = rest_slots(iota((1, PS), 1))
    slot_row = key_of(me_z, bg_, bs_)

    for s in range(MAIN):
        pass_on(l_first, l_pass, s)

    xA.recv()
    w.sC[...] = dot(to_gsz, w.rA[...].reshape(places, W)).astype(BF).reshape(NG, MAIN, NZ, W)
    xC.start()
    w.rC[pl.ds(me_g, 1)] = w.sC[pl.ds(me_g, 1)]

    xB.recv()
    flat = w.rB[...].reshape(PB, Q)
    hits = (slot_col == held_row) & (az_ == lz)
    for r in range(R):
        got = dot(hot(hits & (lrr == r)), flat)
        w.sE[:, :, :, r * Q:(r + 1) * Q] = got.astype(BF).reshape(NG, REST, NZ, Q)
    xE.start()
    w.rE[pl.ds(me_g, 1)] = w.sE[pl.ds(me_g, 1)]

    xz.recv()
    w.ag[...] = jnp.sum(w.azr[...], axis=0, keepdims=True)
    xg.start()
    w.agr[pl.ds(me_g, 1)] = w.ag[...]

    for s in range(MAIN, CAP):
        pass_on(l_first, l_pass, s)

    def own_cols(buf, s, at):
        rows = [buf[:, s, :, r * Q:(r + 1) * Q].reshape(NG * NZ, Q) for r in range(R)]
        cols = dot(w.pi[...], jnp.concatenate(rows, axis=0)).astype(BF)
        w.gown[at] = cols
        w.gfull[at, :, pl.ds(shard_rows(t), Q)] = cols
        for d in (0, 1):
            g_first(at, d).start()

    xC.recv()
    for s in range(MAIN):
        own_cols(w.rC, s, s)
    xE.recv()
    for s in range(REST):
        own_cols(w.rE, s, MAIN + s)

    xg.recv()
    w.ax[...] = jnp.sum(w.agr[...], axis=0, keepdims=True)
    xx.start()
    w.axr[pl.ds(t, 1)] = w.ax[...]

    for s in range(MAIN):
        pass_on(g_first, g_pass, s)

    def precond(s):
        l_own(s).wait()
        local(rr.at[s], w.rv.at[s], w.l_rv.at[s]).wait()
        for d in (0, 1):
            l_pass(s, d).wait_recv()
            g_pass(s, d).wait_recv()
        turned_cols = dot(w.gfull[s], w.rv[s]).astype(BF)
        out = dot(w.lfull[s], turned_cols)
        w.pre[s] = out
        return jnp.sum(jnp.sum(out * out, axis=0, keepdims=True), axis=1, keepdims=True)

    def norms(slots, buf):
        row = jnp.zeros((1, LANES), F32)
        for s in slots:
            row = jnp.where(lane == s, precond(s), row)
        buf[...] = row[None]

    norms(range(MAIN), w.pa)
    xpa.start()
    w.par[pl.ds(t, 1)] = w.pa[...]
    for s in range(MAIN, CAP):
        pass_on(g_first, g_pass, s)

    xx.recv()
    adam_all = jnp.sum(w.axr[...], axis=0)

    def scaled(slots, sums, dest):
        pre_all = jnp.sum(sums[...], axis=0)
        for k, s in enumerate(slots):
            adam_sum = jnp.sum(jnp.where(lane == me_g * 8 + s, adam_all, 0.0), axis=1, keepdims=True)
            pre_sum = jnp.sum(jnp.where(lane == s, pre_all, 0.0), axis=1, keepdims=True)
            scale = jnp.sqrt(adam_sum) / (jnp.sqrt(pre_sum) + 1e-06)
            moved = dot(w.pit[...], (w.pre[s] * scale).astype(BF)).astype(BF)
            for r in range(R):
                part = moved[r * NG * NZ:(r + 1) * NG * NZ].reshape(NG, NZ, Q)
                dest[:, k, :, r * Q:(r + 1) * Q] = part

    xpa.recv()
    scaled(range(MAIN), w.par, w.sF)
    xF.start()
    w.rF[pl.ds(me_g, 1)] = w.sF[pl.ds(me_g, 1)]

    norms(range(MAIN, CAP), w.pb)
    xpb.start()
    w.pbr[pl.ds(t, 1)] = w.pb[...]

    xF.recv()
    w.sI[...] = dot(to_zsg, w.rF[...].reshape(places, W)).astype(BF).reshape(NZ, MAIN * NG, W)
    xI.start()
    w.rI[pl.ds(me_z, 1)] = w.sI[pl.ds(me_z, 1)]

    xpb.recv()
    scaled(range(MAIN, CAP), w.pbr, w.sH)
    xH.start()
    w.rH[pl.ds(me_g, 1)] = w.sH[pl.ds(me_g, 1)]

    def factor(s):
        local(lf.at[s], w.lfv.at[s], w.l_lf.at[s]).wait()
        local(rf.at[s], w.rfv.at[s], w.l_rf.at[s]).wait()
        rows = w.gfull[s, pl.ds(shard_rows(t), Q), :]
        gram = lax.dot_general(rows, w.gfull[s], (((1,), (1,)), ((), ())), preferred_element_type=F32)
        w.lnv[s] = (0.9 * w.lfv[s].astype(F32) + 0.1 * gram).astype(BF)
        local(w.lnv.at[s], ln.at[s], w.l_ln.at[s]).start()
        gram = lax.dot_general(w.gown[s], w.gfull[s], (((0,), (0,)), ((), ())), preferred_element_type=F32)
        w.rnv[s] = (0.9 * w.rfv[s].astype(F32) + 0.1 * gram).astype(BF)
        local(w.rnv.at[s], rn.at[s], w.l_rn.at[s]).start()

    for s in range(MAIN):
        factor(s)

    xH.recv()
    flat = [w.rH[:, :, :, r * Q:(r + 1) * Q].reshape(PS, Q) for r in range(R)]
    hits = (held_col == slot_row) & (mz == bz_)
    total = jnp.zeros((PB, Q), F32)
    for r in range(R):
        total += dot(hot(hits & (mr == r)), flat[r])
    w.sJ[...] = total.astype(BF).reshape(NZ, R * CB, Q)
    xJ.start()
    w.rJ[pl.ds(me_z, 1)] = w.sJ[pl.ds(me_z, 1)]

    for s in range(MAIN, CAP):
        factor(s)

    sel_back = hot(key_col == key_main(iota((1, places), 1)))
    xI.recv()
    xJ.recv()
    rest = w.rJ[...].reshape(PB, Q)
    for r in range(R):
        out = dot(sel_back, w.rI[:, :, r * Q:(r + 1) * Q].reshape(places, Q))
        out += dot(hot(rest_col == jnp.where(lrr == r, l_rest, -2)), rest)
        upd[:, r, :, :] = out.astype(BF).reshape(c.NBR, c.NBC, Q)

    for x in (xA, xB, xz, xC, xE, xg, xx, xpa, xpb, xF, xH, xI, xJ):
        x.sent()
    for s in range(CAP):
        for d in (0, 1):
            for copy in (l_first(s, d), l_pass(s, d), g_first(s, d), g_pass(s, d)):
                copy.wait_send()
        local(w.lnv.at[s], ln.at[s], w.l_ln.at[s]).wait()
        local(w.rnv.at[s], rn.at[s], w.l_rn.at[s]).wait()


def per_device(c, grads, second_moment, owner, left_factor, right_factor, left_root, right_root):
    scratch = scratch_of(c)
    vmem, anyw = pl.BlockSpec(memory_space=pltpu.VMEM), pl.BlockSpec(memory_space=pl.ANY)
    like = lambda a: jax.ShapeDtypeStruct(a.shape, a.dtype)
    return pl.pallas_call(
        functools.partial(kernel, c, tuple(scratch)),
        out_shape=(like(grads), like(second_moment), like(left_factor), like(right_factor)),
        in_specs=[vmem, vmem, vmem, anyw, anyw, anyw, anyw],
        out_specs=(vmem, vmem, anyw, anyw),
        scratch_shapes=list(scratch.values()),
        compiler_params=pltpu.CompilerParams(
            collective_id=c.cid, has_side_effects=True, vmem_limit_bytes=48 * 1024 * 1024
        ),
        name="shampoo",
    )(grads, second_moment, owner, left_factor, right_factor, left_root, right_root)


def build(mesh, body):
    rows, cols = P(None, "fsdp", None, "tp"), P("fsdp", "tp", None)
    return jax.shard_map(
        body, mesh=mesh,
        in_specs=(rows, rows, P(), cols, cols, cols, P("fsdp", None, "tp")),
        out_specs=(rows, rows, cols, cols), check_vma=False,
    )


def solution(mesh):
    c = cfg_of(4, 16, 2, 4, 4, 128, 16, 16, 24, 1)
    return build(mesh, functools.partial(per_device, c))
```

time: 344 us -> 131 us (0.38)
  blocking collectives: 160 us -> 0 us
  waiting for transfers between devices: 129 us -> 0 us
  Pallas kernels: 0 us -> 120 us
  starting transfers between devices: 17.7 us -> 0 us
  between operations: 14.2 us -> 0.66 us
  matrix products: 12.6 us -> 0 us
    pallas_call x0 -> x1, Pallas kernels: none -> 120 us  [per_device(): pl.pallas_call(functools.partial(kernel, c, tuple(scratch)), out_shape=(l...]
    psum x1 -> x0, blocking collectives: 101 us -> none  [per_device(): adam_sums, pre_sums = lax.psum((adam_part, pre_part), ('fsdp', 'tp'))]
    all_gather x2 -> x0, waiting for transfers between devices: 81.4 us -> none  [the longest x1 46 us: per_device(): rotated_whole = lax.all_gather(rotated, 'tp', axis=1, tiled=True)]
    all_to_all x1 -> x0, blocking collectives: 58.6 us -> none  [per_device(): lax.all_to_all(send_pieces, 'fsdp', split_axis=0, concat_axis=2, tiled=True)]
    all_to_all x1 -> x0, waiting for transfers between devices: 47.8 us -> none  [per_device(): lax.all_to_all(sectioned, 'fsdp', split_axis=2, concat_axis=0, tiled=True)]
    all_to_all x1 -> x0, starting transfers between devices: 17.7 us -> none  [per_device(): lax.all_to_all(sectioned, 'fsdp', split_axis=2, concat_axis=0, tiled=True)]
    dot_general x6 -> x0, matrix products: 12.6 us -> none  [the longest x1 3.66 us: per_device(): jnp.einsum('sic,sjc->sij', own_rows, full_block, preferred_element_type=j...]
    unnamed x13 -> x18, local copies, waits for them, and re-layouts: 0.76 us -> 10 us
  transfers between devices with their start and end apart: 3 -> 0, of which waited for: 3 -> 0; matrix products, arithmetic and copies ran while one was open for 2% -> 0% of each run, Pallas kernels for 0% -> 0%
where the time goes in v1:
time: 131 us
  Pallas kernels  120 us (92%)
  local copies, waits for them, and re-layouts  10 us (8%)
    pallas_call x1, Pallas kernels, per_device(): pl.pallas_call(functools.partial(kernel, c, tuple(scratch)), out_shape=(l...  120 us
    unnamed x18, local copies, waits for them, and re-layouts  10 us

profile of v1, /device:TPU:1, one launch (start us, length us, event | category | flops | bytes accessed | tf_op | source)
XLA Modules:
  0.0 130.7 jit_solution(12842684340019236254)
XLA Ops:
  0.6 0.0 copy-start
  0.6 1.1 copy-done
  1.7 0.0 copy-start.1
  1.7 1.1 copy-done.1
  2.8 0.0 copy-start.2
  2.8 1.1 copy-done.2
  3.9 0.0 copy-start.3
  3.9 1.1 copy-done.3
  5.0 0.0 copy-start.4
  5.0 0.9 copy-done.4
  5.9 0.0 copy-start.5
  5.9 0.9 copy-done.5
  6.9 0.0 copy-start.6
  6.9 0.7 copy-done.6
  7.6 120.0 %shampoo.1 = (bf16[16,4,16,128]{3,2,1,0:T(8,128)(2,1)S(1)}, bf16[16,4,16,128]{3,2,1,0:T(8,128)(2,1)S(1)}, bf16[5,128,512]{2,1,0:T(8,128)(2,1)S(1)}, bf16[5,128,512]{2,1,0:T(8,128)(2,1)S(1)}) custom-call(bf16[16,4,16,128]{3,2,1,0:T(8,128)(2,1)S(1)} %copy-done.4, bf16[16,4,16,128]{3,2,1,0:T(8,128)(2,1)S(1)} %copy-done.5, s32[16,16]{1,0:T(8,128)S(1)} %copy-done.6, ...), custom_call_target="tpu_custom_call" | custom-call | tf_op jit(solution)/shard_map/shampoo/pallas_call | solution.py:490
  127.6 0.7 copy.15
  128.3 0.7 copy.16
  129.0 0.8 copy.17
  129.9 0.8 copy.18
Async XLA Ops:
  0.6 1.1 copy-start
  1.7 1.1 copy-start.1
  2.8 1.1 copy-start.2
  3.9 1.1 copy-start.3
  5.0 0.9 copy-start.4
  5.9 0.9 copy-start.5
  6.9 0.7 copy-start.6

commit v2 on v1

--- a/solution.py
+++ b/solution.py
@@ -14,6 +14,7 @@
 MAIN = 2
 REST = CAP - MAIN
 LANES = 128
+VMEM_BYTES = 62 * 1024 * 1024
 
 
 def cfg_of(NY, NZ, NC, NX, R, Q, NBR, NBC, CB, cid):
@@ -26,10 +27,13 @@
     return c
 
 
-def idiv(x, d):
+def idiv(x, d, bound=4096):
     if d & (d - 1) == 0:
         return lax.shift_right_logical(x, jnp.int32(d.bit_length() - 1))
-    return lax.shift_right_logical(x * jnp.int32(-(-(1 << 16) // d)), jnp.int32(16))
+    shift = ((1 << 31) // bound * d).bit_length() - 2
+    factor = -(-(1 << shift) // d)
+    assert bound * factor < 1 << 31 and (factor * d - (1 << shift)) * bound < 1 << shift
+    return lax.shift_right_logical(x * jnp.int32(factor), jnp.int32(shift))
 
 
 def imod(x, d):
@@ -57,44 +61,66 @@
     out = {}
     for name in ("sA", "rA", "sI", "rI"):
         out[name] = vm(c.NZ, MAIN * c.NG, c.W)
-    for name in ("sB", "rB", "sJ", "rJ"):
+    out["zb"] = vm(c.NG, c.NX, c.NZ, c.R * c.CB, c.Q)
+    for name in ("sB", "sJ", "rJ"):
         out[name] = vm(c.NZ, c.R * c.CB, c.Q)
     for name in ("sC", "rC", "sF", "rF"):
         out[name] = vm(c.NG, MAIN, c.NZ, c.W)
-    for name in ("sE", "rE", "sH", "rH"):
+    for name in ("sH", "rH"):
         out[name] = vm(c.NG, REST, c.NZ, c.W)
-    out["gown"] = vm(CAP, c.B, c.Q)
+    out["pick"] = vm(REST * (c.B // c.NY), c.NC * c.NZ * c.R * c.CB)
+    out["gown"] = vm(MAIN, c.B, c.Q)
     out["gfull"] = vm(CAP, c.B, c.B)
     out["lfull"] = vm(CAP, c.B, c.B)
     out["rv"] = vm(CAP, c.B, c.Q)
     for name in ("lfv", "rfv", "lnv", "rnv"):
         out[name] = vm(CAP, c.Q, c.B)
-    out["pre"] = vf(CAP, c.B, c.Q)
     out["pi"] = vm(c.B, c.B)
     out["pit"] = vm(c.B, c.B)
     out["az"] = vf(c.NZ, 1, LANES)
     out["azr"] = vf(c.NZ, 1, LANES)
-    out["ag"] = vf(1, 1, LANES)
-    out["agr"] = vf(c.NG, 1, LANES)
-    for name in ("ax", "pa", "pb"):
+    out["wz"] = vf(1, 1, LANES)
+    out["wzr"] = vf(c.NZ, 1, LANES)
+    for name in ("ag", "wg"):
+        out[name] = vf(1, 1, LANES)
+        out[name + "r"] = vf(c.NG, 1, LANES)
+    for name in ("ax", "pa"):
         out[name] = vf(1, 1, LANES)
         out[name + "r"] = vf(c.NX, 1, LANES)
-    for name in ("A", "B", "I", "J", "z"):
+    for name in ("A", "B", "I", "J", "z", "wz"):
         out["s_" + name], out["r_" + name] = dma(c.NZ), dma(c.NZ)
-    for name in ("C", "E", "F", "H", "g"):
+    for name in ("C", "F", "H", "g", "wg"):
         out["s_" + name], out["r_" + name] = dma(c.NG), dma(c.NG)
-    for name in ("x", "pa", "pb"):
+    for name in ("x", "pa"):
         out["s_" + name], out["r_" + name] = dma(c.NX), dma(c.NX)
     for name in ("L1", "L2", "G1", "G2"):
         out["s_" + name], out["r_" + name] = dma(CAP, 2), dma(CAP, 2)
+    for name in ("X1", "X2", "Y1", "Y2"):
+        out["s_" + name], out["r_" + name] = dma(2), dma(2)
+    out["s_K"], out["r_K"] = dma(c.NY), dma(c.NY)
     for name in ("l_lf", "l_rf", "l_rv", "l_lr", "l_ln", "l_rn"):
         out[name] = dma(CAP)
+    out["upd"] = vm(c.NBR, c.R, c.NBC, c.Q)
+    out["mom"] = vm(c.NBR, c.R, c.NBC, c.Q)
+    out["l_out"] = dma(2)
+    out["grads"] = vm(c.NBR, c.R, c.NBC, c.Q)
+    out["sm"] = vm(c.NBR, c.R, c.NBC, c.Q)
+    out["owner"] = pltpu.VMEM((c.NBR, c.NBC), I32)
+    out["l_in"] = dma(3)
     return out
 
 
-def kernel(c, names, grads, sm, owner, lf, rf, lr, rr, upd, mom, ln, rn, *scratch):
+def kernel(c, names, grads_in, sm_in, owner_in, lf, rf, lr, rr, upd_out, mom_out, ln, rn, left_out, *scratch):
     w = types.SimpleNamespace(**dict(zip(names, scratch)))
     NZ, NG, NX, NB, R, Q, B, W, CB = c.NZ, c.NG, c.NX, c.NB, c.R, c.Q, c.B, c.W, c.CB
+    grads, sm, owner, upd, mom = w.grads, w.sm, w.owner, w.upd, w.mom
+    outputs = [pltpu.make_async_copy(mom, mom_out, w.l_out.at[0]), pltpu.make_async_copy(upd, upd_out, w.l_out.at[1])]
+    inputs = [
+        pltpu.make_async_copy(a, b, w.l_in.at[k])
+        for k, (a, b) in enumerate(((owner_in, owner), (grads_in, grads), (sm_in, sm)))
+    ]
+    for copy in inputs:
+        copy.start()
     f = lax.axis_index("fsdp")
     t = lax.axis_index("tp")
     me_c = lax.rem(f, c.NC)
@@ -166,18 +192,18 @@
         return lambda p: buf.at[p]
 
     xA = Exchange(each_z, at_z, me_z, many(w.sA), w.rA, "A")
-    xB = Exchange(each_z, at_z, me_z, many(w.sB), w.rB, "B")
+    xB = Exchange(each_z, at_z, me_z, many(w.sB), w.zb.at[me_g, t], "B")
     xI = Exchange(each_z, at_z, me_z, many(w.sI), w.rI, "I")
     xJ = Exchange(each_z, at_z, me_z, many(w.sJ), w.rJ, "J")
     xz = Exchange(each_z, at_z, me_z, many(w.az), w.azr, "z")
     xC = Exchange(each_g, at_g, me_g, many(w.sC), w.rC, "C")
-    xE = Exchange(each_g, at_g, me_g, many(w.sE), w.rE, "E")
     xF = Exchange(each_g, at_g, me_g, many(w.sF), w.rF, "F")
     xH = Exchange(each_g, at_g, me_g, many(w.sH), w.rH, "H")
     xg = Exchange(each_g, at_g, me_g, one(w.ag), w.agr, "g")
     xx = Exchange(each_x, at_x, t, one(w.ax), w.axr, "x")
     xpa = Exchange(each_x, at_x, t, one(w.pa), w.par, "pa")
-    xpb = Exchange(each_x, at_x, t, one(w.pb), w.pbr, "pb")
+    xwg = Exchange(each_g, at_g, me_g, one(w.wg), w.wgr, "wg")
+    xwz = Exchange(each_z, at_z, me_z, one(w.wz), w.wzr, "wz")
 
     def shard_rows(x):
         return pl.multiple_of(x * Q, Q)
@@ -200,10 +226,41 @@
         part = w.gfull.at[s, pl.ds(d * (B // 2), B // 2), pl.ds(shard_rows(x), Q)]
         return rcopy(part, part, w.s_G2.at[s, d], w.r_G2.at[s, d], at_x(right if d == 0 else left))
 
-    def pass_on(first, onward, s):
+    def pass_on(first, onward, *s):
         for d in (0, 1):
-            first(s, d).wait_recv()
-            onward(s, d).start()
+            first(*s, d).wait_recv()
+            onward(*s, d).start()
+
+    up, down = lax.rem(me_y + 1, c.NY), lax.rem(me_y + c.NY - 1, c.NY)
+
+    def b_copy(part, name, k, dev):
+        sems = getattr(w, "s_" + name), getattr(w, "r_" + name)
+        return rcopy(part, part, sems[0].at[k], sems[1].at[k], dev)
+
+    def bx_first(d):
+        return b_copy(w.zb.at[me_g, t], "X1", d, at_x(right if d == 0 else left))
+
+    def bx_pass(d):
+        part = w.zb.at[me_g, left if d == 0 else right, pl.ds(d * (NZ // 2), NZ // 2)]
+        return b_copy(part, "X2", d, at_x(right if d == 0 else left))
+
+    def at_y(y):
+        return at_g(y * c.NC + me_c)
+
+    def by_first(d):
+        return b_copy(w.zb.at[me_g], "Y1", d, at_y(up if d == 0 else down))
+
+    def by_pass(d):
+        part = w.zb.at[(down if d == 0 else up) * c.NC + me_c, pl.ds(d * (NX // 2), NX // 2)]
+        return b_copy(part, "Y2", d, at_y(up if d == 0 else down))
+
+    def b_core(k):
+        y = lax.rem(me_y + k, c.NY)
+        return b_copy(w.zb.at[y * c.NC + me_c], "K", k, at_g(me_y * c.NC + (1 - me_c)))
+
+    def b_core_in(k):
+        y = lax.rem(me_y + k, c.NY)
+        return b_copy(w.zb.at[y * c.NC + (1 - me_c)], "K", k, at_g(me_y * c.NC + (1 - me_c)))
 
     barrier = pltpu.get_barrier_semaphore()
 
@@ -228,6 +285,7 @@
             local(rf.at[s], w.rfv.at[s], w.l_rf.at[s]),
         )
 
+    inputs[0].wait()
     spread = hot(imod(iota((c.NBC, NB), 1), c.NBC) == iota((c.NBC, NB), 0))
     wide = dot(owner[...].astype(F32).astype(BF), spread)
     own_row = jnp.sum(
@@ -250,6 +308,7 @@
 
     places = NZ * MAIN * NG
     sel_main = hot(key_main(iota((places, 1), 0)) == key_row)
+    inputs[1].wait()
     for r in range(R):
         block = grads[:, r, :, :].reshape(NB, Q)
         w.sA[:, :, r * Q:(r + 1) * Q] = dot(sel_main, block).astype(BF).reshape(NZ, MAIN * NG, Q)
@@ -265,6 +324,7 @@
     pos_row = jnp.sum(jnp.where(mates & over_col & (i0 < i1), 1.0, 0.0), axis=0, keepdims=True).astype(I32)
     pos_col = jnp.sum(jnp.where(mates & over_row & (i1 < i0), 1.0, 0.0), axis=1, keepdims=True).astype(I32)
     PB = NZ * R * CB
+    left_out[0] = jnp.sum(jnp.where(over_row & (pos_row >= CB), 1, 0))
     rest_row = jnp.where(over_row & (pos_row < CB), z_row * CB + pos_row, -1)
     rest_col = jnp.where(over_col & (pos_col < CB), z_col * CB + pos_col, -1)
 
@@ -281,15 +341,13 @@
     w.sB[...] = total.astype(BF).reshape(NZ, R * CB, Q)
     xB.start()
     w.rA[pl.ds(me_z, 1)] = w.sA[pl.ds(me_z, 1)]
-    w.rB[pl.ds(me_z, 1)] = w.sB[pl.ds(me_z, 1)]
-    for s in range(MAIN, CAP):
-        for d in (0, 1):
-            l_first(s, d).start()
+    w.zb[pl.ds(me_g, 1), pl.ds(t, 1), pl.ds(me_z, 1)] = w.sB[pl.ds(me_z, 1)][None, None]
     for s in range(CAP):
         l_own(s).start()
         for copy in loads(s):
             copy.start()
 
+    inputs[2].wait()
     adam_col = jnp.zeros((NB, 1), F32)
     for r in range(R):
         g = grads[:, r, :, :].astype(F32)
@@ -297,6 +355,7 @@
         mom[:, r, :, :] = moment.astype(BF)
         adam = g / (jnp.sqrt(moment) + 1e-08)
         adam_col += jnp.sum((adam * adam).reshape(NB, Q), axis=1, keepdims=True)
+    outputs[0].start()
     lane = iota((1, LANES), 1)
     lane_key = jnp.where(lane < NG * 8, key_of(jnp.zeros_like(lane), idiv(lane, 8), imod(lane, 8)), -1)
 
@@ -318,8 +377,11 @@
     to_gsz = hot(turned(iota((places, 1), 0)) == iota((places, places), 1))
     to_zsg = hot(iota((places, places), 0) == turned(iota((1, places), 1)))
 
+    gm = iota((1, c.NC * PB), 1)
+    gc = idiv(gm, PB)
+    gz, gr, gb = rest_parts(gm - gc * PB)
     held_row = jnp.sum(
-        jnp.where(rest_col == me_z * CB + lb, key_col + 1, 0), axis=0, keepdims=True
+        jnp.where(rest_col == me_z * CB + gb, key_col + 1, 0), axis=0, keepdims=True
     ) - 1
     held_col = jnp.sum(
         jnp.where(me_z * CB + mb == rest_row, key_row + 1, 0), axis=1, keepdims=True
@@ -328,115 +390,123 @@
     def rest_slots(m):
         return idiv(m, REST * NZ), imod(idiv(m, NZ), REST) + MAIN, imod(m, NZ)
     PS = NG * REST * NZ
-    ag_, as_, az_ = rest_slots(iota((PS, 1), 0))
-    slot_col = key_of(me_z, ag_, as_)
     bg_, bs_, bz_ = rest_slots(iota((1, PS), 1))
     slot_row = key_of(me_z, bg_, bs_)
 
+    per_y = c.B // c.NY
+    n = iota((REST * per_y, 1), 0)
+    slot = idiv(n, per_y)
+    n = n - slot * per_y
+    n_z, n_c, n_r = idiv(n, c.NC * R), imod(idiv(n, R), c.NC), imod(n, R)
+    wanted = key_of(me_z, me_g, slot + MAIN)
+    w.pick[...] = hot((held_row == wanted) & (gz == n_z) & (gc == n_c) & (gr == n_r))
     for s in range(MAIN):
         pass_on(l_first, l_pass, s)
 
+    for s in range(MAIN, CAP):
+        for d in (0, 1):
+            l_first(s, d).start()
     xA.recv()
     w.sC[...] = dot(to_gsz, w.rA[...].reshape(places, W)).astype(BF).reshape(NG, MAIN, NZ, W)
     xC.start()
     w.rC[pl.ds(me_g, 1)] = w.sC[pl.ds(me_g, 1)]
 
     xB.recv()
-    flat = w.rB[...].reshape(PB, Q)
-    hits = (slot_col == held_row) & (az_ == lz)
-    for r in range(R):
-        got = dot(hot(hits & (lrr == r)), flat)
-        w.sE[:, :, :, r * Q:(r + 1) * Q] = got.astype(BF).reshape(NG, REST, NZ, Q)
-    xE.start()
-    w.rE[pl.ds(me_g, 1)] = w.sE[pl.ds(me_g, 1)]
+    for d in (0, 1):
+        bx_first(d).start()
+
+    xC.recv()
+    for s in range(MAIN):
+        rows = [w.rC[:, s, :, r * Q:(r + 1) * Q].reshape(NG * NZ, Q) for r in range(R)]
+        cols = dot(w.pi[...], jnp.concatenate(rows, axis=0)).astype(BF)
+        w.gown[s] = cols
+        w.gfull[s, :, pl.ds(shard_rows(t), Q)] = cols
+    pass_on(bx_first, bx_pass)
+    for s in range(MAIN):
+        for d in (0, 1):
+            g_first(s, d).start()
+
+    for d in (0, 1):
+        bx_pass(d).wait_recv()
+    for d in (0, 1):
+        by_first(d).start()
+    b_core(0).start()
+
+    for s in range(MAIN):
+        pass_on(g_first, g_pass, s)
+
+    for s in range(MAIN, CAP):
+        pass_on(l_first, l_pass, s)
+
+    pass_on(by_first, by_pass)
+    b_core(1).start()
+    b_core(c.NY - 1).start()
+
+    norm_row = jnp.zeros((1, LANES), F32)
+
+    def precond(s, dest, at):
+        l_own(s).wait()
+        local(rr.at[s], w.rv.at[s], w.l_rv.at[s]).wait()
+        for d in (0, 1):
+            l_pass(s, d).wait_recv()
+            if s < MAIN:
+                g_pass(s, d).wait_recv()
+        cols = dot(w.gfull[s], w.rv[s])
+        high = cols.astype(BF)
+        low = (cols - high.astype(F32)).astype(BF)
+        out = (dot(w.lfull[s], high) + dot(w.lfull[s], low)).astype(BF)
+        moved = dot(w.pit[...], out).astype(BF)
+        for r in range(R):
+            dest[:, at, :, r * Q:(r + 1) * Q] = moved[r * NG * NZ:(r + 1) * NG * NZ].reshape(NG, NZ, Q)
+        wide_out = out.astype(F32)
+        total = jnp.sum(jnp.sum(wide_out * wide_out, axis=0, keepdims=True), axis=1, keepdims=True)
+        return jnp.where(lane == s, total, norm_row)
+
+    for s in range(MAIN):
+        norm_row = precond(s, w.sF, s)
+    xF.start()
+    w.rF[pl.ds(me_g, 1)] = w.sF[pl.ds(me_g, 1)]
+
+    for d in (0, 1):
+        by_pass(d).wait_recv()
+    b_core(2).start()
 
     xz.recv()
     w.ag[...] = jnp.sum(w.azr[...], axis=0, keepdims=True)
     xg.start()
     w.agr[pl.ds(me_g, 1)] = w.ag[...]
 
+    for k in range(c.NY):
+        b_core_in(k).wait_recv()
+
+    def place(y):
+        parts = [
+            jnp.concatenate([w.zb[y * c.NC + k, x].reshape(PB, Q) for x in range(NX)], axis=1)
+            for k in range(c.NC)
+        ]
+        got = dot(w.pick[...], jnp.concatenate(parts, axis=0)).astype(BF)
+        for k in range(REST):
+            rows = pl.ds(pl.multiple_of(y * per_y, per_y), per_y)
+            w.gfull[MAIN + k, rows, :] = got[k * per_y:(k + 1) * per_y]
+    loop(0, c.NY, place)
+
+    xF.recv()
+    w.sI[...] = dot(to_zsg, w.rF[...].reshape(places, W)).astype(BF).reshape(NZ, MAIN * NG, W)
+    xI.start()
+    w.rI[pl.ds(me_z, 1)] = w.sI[pl.ds(me_z, 1)]
+
     for s in range(MAIN, CAP):
-        pass_on(l_first, l_pass, s)
-
-    def own_cols(buf, s, at):
-        rows = [buf[:, s, :, r * Q:(r + 1) * Q].reshape(NG * NZ, Q) for r in range(R)]
-        cols = dot(w.pi[...], jnp.concatenate(rows, axis=0)).astype(BF)
-        w.gown[at] = cols
-        w.gfull[at, :, pl.ds(shard_rows(t), Q)] = cols
-        for d in (0, 1):
-            g_first(at, d).start()
-
-    xC.recv()
-    for s in range(MAIN):
-        own_cols(w.rC, s, s)
-    xE.recv()
-    for s in range(REST):
-        own_cols(w.rE, s, MAIN + s)
+        norm_row = precond(s, w.sH, s - MAIN)
+    xH.start()
+    w.rH[pl.ds(me_g, 1)] = w.sH[pl.ds(me_g, 1)]
+    w.pa[...] = norm_row[None]
+    xpa.start()
+    w.par[pl.ds(t, 1)] = w.pa[...]
 
     xg.recv()
     w.ax[...] = jnp.sum(w.agr[...], axis=0, keepdims=True)
     xx.start()
     w.axr[pl.ds(t, 1)] = w.ax[...]
-
-    for s in range(MAIN):
-        pass_on(g_first, g_pass, s)
-
-    def precond(s):
-        l_own(s).wait()
-        local(rr.at[s], w.rv.at[s], w.l_rv.at[s]).wait()
-        for d in (0, 1):
-            l_pass(s, d).wait_recv()
-            g_pass(s, d).wait_recv()
-        turned_cols = dot(w.gfull[s], w.rv[s]).astype(BF)
-        out = dot(w.lfull[s], turned_cols)
-        w.pre[s] = out
-        return jnp.sum(jnp.sum(out * out, axis=0, keepdims=True), axis=1, keepdims=True)
-
-    def norms(slots, buf):
-        row = jnp.zeros((1, LANES), F32)
-        for s in slots:
-            row = jnp.where(lane == s, precond(s), row)
-        buf[...] = row[None]
-
-    norms(range(MAIN), w.pa)
-    xpa.start()
-    w.par[pl.ds(t, 1)] = w.pa[...]
-    for s in range(MAIN, CAP):
-        pass_on(g_first, g_pass, s)
-
-    xx.recv()
-    adam_all = jnp.sum(w.axr[...], axis=0)
-
-    def scaled(slots, sums, dest):
-        pre_all = jnp.sum(sums[...], axis=0)
-        for k, s in enumerate(slots):
-            adam_sum = jnp.sum(jnp.where(lane == me_g * 8 + s, adam_all, 0.0), axis=1, keepdims=True)
-            pre_sum = jnp.sum(jnp.where(lane == s, pre_all, 0.0), axis=1, keepdims=True)
-            scale = jnp.sqrt(adam_sum) / (jnp.sqrt(pre_sum) + 1e-06)
-            moved = dot(w.pit[...], (w.pre[s] * scale).astype(BF)).astype(BF)
-            for r in range(R):
-                part = moved[r * NG * NZ:(r + 1) * NG * NZ].reshape(NG, NZ, Q)
-                dest[:, k, :, r * Q:(r + 1) * Q] = part
-
-    xpa.recv()
-    scaled(range(MAIN), w.par, w.sF)
-    xF.start()
-    w.rF[pl.ds(me_g, 1)] = w.sF[pl.ds(me_g, 1)]
-
-    norms(range(MAIN, CAP), w.pb)
-    xpb.start()
-    w.pbr[pl.ds(t, 1)] = w.pb[...]
-
-    xF.recv()
-    w.sI[...] = dot(to_zsg, w.rF[...].reshape(places, W)).astype(BF).reshape(NZ, MAIN * NG, W)
-    xI.start()
-    w.rI[pl.ds(me_z, 1)] = w.sI[pl.ds(me_z, 1)]
-
-    xpb.recv()
-    scaled(range(MAIN, CAP), w.pbr, w.sH)
-    xH.start()
-    w.rH[pl.ds(me_g, 1)] = w.sH[pl.ds(me_g, 1)]
-
     def factor(s):
         local(lf.at[s], w.lfv.at[s], w.l_lf.at[s]).wait()
         local(rf.at[s], w.rfv.at[s], w.l_rf.at[s]).wait()
@@ -444,12 +514,27 @@
         gram = lax.dot_general(rows, w.gfull[s], (((1,), (1,)), ((), ())), preferred_element_type=F32)
         w.lnv[s] = (0.9 * w.lfv[s].astype(F32) + 0.1 * gram).astype(BF)
         local(w.lnv.at[s], ln.at[s], w.l_ln.at[s]).start()
-        gram = lax.dot_general(w.gown[s], w.gfull[s], (((0,), (0,)), ((), ())), preferred_element_type=F32)
+        cols = w.gfull[s, :, pl.ds(shard_rows(t), Q)]
+        gram = lax.dot_general(cols, w.gfull[s], (((0,), (0,)), ((), ())), preferred_element_type=F32)
         w.rnv[s] = (0.9 * w.rfv[s].astype(F32) + 0.1 * gram).astype(BF)
         local(w.rnv.at[s], rn.at[s], w.l_rn.at[s]).start()
 
     for s in range(MAIN):
         factor(s)
+
+    xx.recv()
+    xpa.recv()
+    adam_all = jnp.sum(w.axr[...], axis=0)
+    norm_all = jnp.sum(w.par[...], axis=0)
+    scales = jnp.zeros((1, LANES), F32)
+    for s in range(CAP):
+        adam_sum = jnp.sum(jnp.where(lane == me_g * 8 + s, adam_all, 0.0), axis=1, keepdims=True)
+        norm_sum = jnp.sum(jnp.where(lane == s, norm_all, 0.0), axis=1, keepdims=True)
+        scale = jnp.sqrt(adam_sum) / (jnp.sqrt(norm_sum) + 1e-06)
+        scales = jnp.where(lane == me_g * 8 + s, scale, scales)
+    w.wg[...] = scales[None]
+    xwg.start()
+    w.wgr[pl.ds(me_g, 1)] = w.wg[...]
 
     xH.recv()
     flat = [w.rH[:, :, :, r * Q:(r + 1) * Q].reshape(PS, Q) for r in range(R)]
@@ -461,43 +546,104 @@
     xJ.start()
     w.rJ[pl.ds(me_z, 1)] = w.sJ[pl.ds(me_z, 1)]
 
+    xwg.recv()
+    w.wz[...] = jnp.sum(w.wgr[...], axis=0, keepdims=True)
+    xwz.start()
+    w.wzr[pl.ds(me_z, 1)] = w.wz[...]
+
     for s in range(MAIN, CAP):
         factor(s)
 
     sel_back = hot(key_col == key_main(iota((1, places), 1)))
     xI.recv()
+    main_part = [dot(sel_back, w.rI[:, :, r * Q:(r + 1) * Q].reshape(places, Q)) for r in range(R)]
+    xwz.recv()
+
+    def scale_of(z, total):
+        return total + jnp.where((key_col - z * (c.NC * 8)) == lane_key, w.wzr[z], 0.0)
+    scale_col = jnp.sum(
+        lax.fori_loop(0, NZ, scale_of, jnp.zeros((NB, LANES), F32)), axis=1, keepdims=True
+    )
     xJ.recv()
     rest = w.rJ[...].reshape(PB, Q)
     for r in range(R):
-        out = dot(sel_back, w.rI[:, :, r * Q:(r + 1) * Q].reshape(places, Q))
-        out += dot(hot(rest_col == jnp.where(lrr == r, l_rest, -2)), rest)
-        upd[:, r, :, :] = out.astype(BF).reshape(c.NBR, c.NBC, Q)
-
-    for x in (xA, xB, xz, xC, xE, xg, xx, xpa, xpb, xF, xH, xI, xJ):
+        out = main_part[r] + dot(hot(rest_col == jnp.where(lrr == r, l_rest, -2)), rest)
+        upd[:, r, :, :] = (out * scale_col).astype(BF).reshape(c.NBR, c.NBC, Q)
+
+    outputs[1].start()
+    for copy in outputs:
+        copy.wait()
+    for x in (xA, xB, xz, xC, xg, xx, xpa, xF, xH, xI, xJ, xwg, xwz):
         x.sent()
+    for d in (0, 1):
+        for copy in (bx_first(d), bx_pass(d), by_first(d), by_pass(d)):
+            copy.wait_send()
+        for s in range(CAP):
+            l_first(s, d).wait_send()
+            l_pass(s, d).wait_send()
+        for s in range(MAIN):
+            g_first(s, d).wait_send()
+            g_pass(s, d).wait_send()
+    for k in range(c.NY):
+        b_core(k).wait_send()
     for s in range(CAP):
-        for d in (0, 1):
-            for copy in (l_first(s, d), l_pass(s, d), g_first(s, d), g_pass(s, d)):
-                copy.wait_send()
         local(w.lnv.at[s], ln.at[s], w.l_ln.at[s]).wait()
         local(w.rnv.at[s], rn.at[s], w.l_rn.at[s]).wait()
 
 
-def per_device(c, grads, second_moment, owner, left_factor, right_factor, left_root, right_root):
+def finish(results):
+    count = len(results)
+
+    def body(*refs):
+        ins, outs, held, (got, put) = refs[:count], refs[count:2 * count], refs[2 * count:3 * count], refs[3 * count:]
+        arrays = list(enumerate(zip(ins, held, outs)))
+        for k, (a, v, _) in arrays:
+            pltpu.make_async_copy(a, v, got.at[k]).start()
+        for k, (a, v, o) in arrays:
+            pltpu.make_async_copy(a, v, got.at[k]).wait()
+            pltpu.make_async_copy(v, o, put.at[k]).start()
+        for k, (_, v, o) in arrays:
+            pltpu.make_async_copy(v, o, put.at[k]).wait()
+    hbm = pl.BlockSpec(memory_space=pltpu.HBM)
+    return tuple(pl.pallas_call(
+        body,
+        out_shape=tuple(jax.ShapeDtypeStruct(a.shape, a.dtype) for a in results),
+        in_specs=[hbm] * count,
+        out_specs=(hbm,) * count,
+        scratch_shapes=[pltpu.VMEM(a.shape, a.dtype) for a in results] + [pltpu.SemaphoreType.DMA((count,))] * 2,
+        compiler_params=pltpu.CompilerParams(vmem_limit_bytes=VMEM_BYTES),
+        name="finish",
+    )(*results))
+
+
+def step(c, grads, second_moment, owner, left_factor, right_factor, left_root, right_root):
     scratch = scratch_of(c)
-    vmem, anyw = pl.BlockSpec(memory_space=pltpu.VMEM), pl.BlockSpec(memory_space=pl.ANY)
+    vmem, hbm = pl.BlockSpec(memory_space=pltpu.VMEM), pl.BlockSpec(memory_space=pltpu.HBM)
+    smem = pl.BlockSpec(memory_space=pltpu.SMEM)
     like = lambda a: jax.ShapeDtypeStruct(a.shape, a.dtype)
     return pl.pallas_call(
         functools.partial(kernel, c, tuple(scratch)),
-        out_shape=(like(grads), like(second_moment), like(left_factor), like(right_factor)),
-        in_specs=[vmem, vmem, vmem, anyw, anyw, anyw, anyw],
-        out_specs=(vmem, vmem, anyw, anyw),
+        out_shape=(
+            like(grads), like(second_moment), like(left_factor), like(right_factor),
+            jax.ShapeDtypeStruct((1,), I32),
+        ),
+        in_specs=[hbm] * 7,
+        out_specs=(hbm, hbm, hbm, hbm, smem),
         scratch_shapes=list(scratch.values()),
         compiler_params=pltpu.CompilerParams(
-            collective_id=c.cid, has_side_effects=True, vmem_limit_bytes=48 * 1024 * 1024
+            collective_id=c.cid, has_side_effects=True, vmem_limit_bytes=VMEM_BYTES
         ),
         name="shampoo",
     )(grads, second_moment, owner, left_factor, right_factor, left_root, right_root)
+
+
+def per_device(few, enough, *args):
+    *results, left_out = step(few, *args)
+    return lax.cond(
+        left_out[0] == 0,
+        lambda: finish(results),
+        lambda: finish(step(enough, *args)[:4]),
+    )
 
 
 def build(mesh, body):
@@ -510,5 +656,6 @@
 
 
 def solution(mesh):
-    c = cfg_of(4, 16, 2, 4, 4, 128, 16, 16, 24, 1)
-    return build(mesh, functools.partial(per_device, c))
+    few = cfg_of(4, 16, 2, 4, 4, 128, 16, 16, 4, 1)
+    enough = cfg_of(4, 16, 2, 4, 4, 128, 16, 16, 24, 2)
+    return build(mesh, functools.partial(per_device, few, enough))

time: 131 us -> 90.8 us (0.69)
  Pallas kernels: 120 us -> 88.7 us
  local copies, waits for them, and re-layouts: 10 us -> 0.03 us
    pallas_call x1 -> x2, Pallas kernels: 120 us -> 88.7 us  [the longest x1 86.4 us: step(): pl.pallas_call(functools.partial(kernel, c, tuple(scratch)), out_shape=(l...]
    unnamed x18 -> x8, local copies, waits for them, and re-layouts: 10 us -> 0.03 us
where the time goes in v2:
time: 90.8 us; the launch traced here: 90.5 us
  Pallas kernels  88.7 us (98%)
  between operations  1.53 us (2%)
    pallas_call x1, Pallas kernels, step(): pl.pallas_call(functools.partial(kernel, c, tuple(scratch)), out_shape=(l...  86.4 us
    pallas_call x1, Pallas kernels, finish(): pl.pallas_call(body, out_shape=tuple((jax.ShapeDtypeStruct(a.shape, a.dty...  2.37 us

profile of v2, /device:TPU:1, one launch (start us, length us, event | category | flops | bytes accessed | tf_op | source)
XLA Modules:
  0.0 90.5 jit_solution(4537403569771100489)
XLA Ops:
  0.6 0.0 copy-start
  0.6 0.0 copy-start.1
  0.7 0.0 copy-start.2
  0.7 86.4 %shampoo.3 = (bf16[16,4,16,128]{3,2,1,0:T(8,128)(2,1)}, bf16[16,4,16,128]{3,2,1,0:T(8,128)(2,1)}, bf16[5,128,512]{2,1,0:T(8,128)(2,1)}, bf16[5,128,512]{2,1,0:T(8,128)(2,1)}, s32[1]{0:T(128)}) custom-call(bf16[16,4,16,128]{3,2,1,0:T(8,128)(2,1)} %grads_in.1, bf16[16,4,16,128]{3,2,1,0:T(8,128)(2,1)} %sm_in.1, s32[16,16]{1,0:T(8,128)} %owner_in.1, ...), custom_call_target="tpu_custom_call" | custom-call | tf_op jit(solution)/shard_map/shampoo/pallas_call | solution.py:624
  87.0 0.0 copy-start.3
  87.7 0.0 copy-done
  87.7 0.0 copy-done.1
  87.7 0.0 copy-done.2
  87.7 0.0 copy-done.3
  87.7 2.6 %conditional.1 = ((bf16[16,4,16,128]{3,2,1,0:T(8,128)(2,1)}, bf16[16,4,16,128]{3,2,1,0:T(8,128)(2,1)}, bf16[5,128,512]{2,1,0:T(8,128)(2,1)}, bf16[5,128,512]{2,1,0:T(8,128)(2,1)})) conditional(s32[]{:T(128)} %bitcast, (bf16[16,4,16,128]{3,2,1,0:T(8,128)(2,1)}, bf16[16,4,16,128]{3,2,1,0:T(8,128)(2,1)}, s32[16,16]{1,0:T(8,128)S(1)}, ...), branch_computations={%region_0.0_spmd, %region_1.0_spmd} | conditional | bytes 8 | solution.py:642
  88.0 2.4 %finish.3 = (bf16[16,4,16,128]{3,2,1,0:T(8,128)(2,1)}, bf16[16,4,16,128]{3,2,1,0:T(8,128)(2,1)}, bf16[5,128,512]{2,1,0:T(8,128)(2,1)}, bf16[5,128,512]{2,1,0:T(8,128)(2,1)}) custom-call(bf16[16,4,16,128]{3,2,1,0:T(8,128)(2,1)} %get-tuple-element.33.refs_0_, bf16[16,4,16,128]{3,2,1,0:T(8,128)(2,1)} %get-tuple-element.34.refs_1_, ...), custom_call_target="tpu_custom_call" | custom-call | tf_op jit(solution)/shard_map/cond/branch_1_fun/finish/pallas_call | solution.py:608
Async XLA Ops:
  0.6 87.1 %copy-start = (bf16[5,128,512]{2,1,0:T(8,128)(2,1)S(1)}, bf16[5,128,512]{2,1,0:T(8,128)(2,1)}, u32[]{:S(2)}) copy-start(bf16[5,128,512]{2,1,0:T(8,128)(2,1)} %lf.1) | copy-start | bytes 1966084
  0.6 87.1 %copy-start.1 = (bf16[5,128,512]{2,1,0:T(8,128)(2,1)S(1)}, bf16[5,128,512]{2,1,0:T(8,128)(2,1)}, u32[]{:S(2)}) copy-start(bf16[5,128,512]{2,1,0:T(8,128)(2,1)} %rf.1) | copy-start | bytes 1966084
  0.7 87.1 %copy-start.2 = (bf16[5,128,512]{2,1,0:T(8,128)(2,1)S(1)}, bf16[5,128,512]{2,1,0:T(8,128)(2,1)}, u32[]{:S(2)}) copy-start(bf16[5,128,512]{2,1,0:T(8,128)(2,1)} %lr.1) | copy-start | bytes 1966084
  87.0 0.7 copy-start.3

commit v3 on v2

--- a/solution.py
+++ b/solution.py
@@ -88,18 +88,18 @@
         out[name] = vf(1, 1, LANES)
         out[name + "r"] = vf(c.NX, 1, LANES)
     for name in ("A", "B", "I", "J", "z", "wz"):
-        out["s_" + name], out["r_" + name] = dma(c.NZ), dma(c.NZ)
+        out["s_" + name], out["r_" + name] = dma(1), dma(1)
     for name in ("C", "F", "H", "g", "wg"):
-        out["s_" + name], out["r_" + name] = dma(c.NG), dma(c.NG)
+        out["s_" + name], out["r_" + name] = dma(1), dma(1)
     for name in ("x", "pa"):
-        out["s_" + name], out["r_" + name] = dma(c.NX), dma(c.NX)
+        out["s_" + name], out["r_" + name] = dma(1), dma(1)
     for name in ("L1", "L2", "G1", "G2"):
         out["s_" + name], out["r_" + name] = dma(CAP, 2), dma(CAP, 2)
     for name in ("X1", "X2", "Y1", "Y2"):
         out["s_" + name], out["r_" + name] = dma(2), dma(2)
     out["s_K"], out["r_K"] = dma(c.NY), dma(c.NY)
     for name in ("l_lf", "l_rf", "l_rv", "l_lr", "l_ln", "l_rn"):
-        out[name] = dma(CAP)
+        out[name] = dma(1)
     out["upd"] = vm(c.NBR, c.R, c.NBC, c.Q)
     out["mom"] = vm(c.NBR, c.R, c.NBC, c.Q)
     out["l_out"] = dma(2)
@@ -168,22 +168,23 @@
     class Exchange:
         def __init__(self, each, at, me, src, dst, sems):
             self.each, self.at, self.me, self.src, self.dst = each, at, me, src, dst
-            self.ss, self.rs = getattr(w, "s_" + sems), getattr(w, "r_" + sems)
+            self.ss, self.rs = getattr(w, "s_" + sems).at[0], getattr(w, "r_" + sems).at[0]
+            self.count = {each_z: NZ, each_g: NG, each_x: NX}[each]
 
         def start(self):
             def go(p):
-                rcopy(self.src(p), self.dst.at[self.me], self.ss.at[p], self.rs.at[self.me], self.at(p)).start()
+                rcopy(self.src(p), self.dst.at[self.me], self.ss, self.rs, self.at(p)).start()
             self.each(go)
 
+        def all(self):
+            whole = self.dst.at[pl.ds(0, self.count - 1)]
+            return rcopy(whole, whole, self.ss, self.rs, self.at(lax.rem(self.me + 1, self.count)))
+
         def recv(self):
-            def go(p):
-                rcopy(self.src(p), self.dst.at[p], self.ss.at[p], self.rs.at[p], self.at(p)).wait_recv()
-            self.each(go)
+            self.all().wait_recv()
 
         def sent(self):
-            def go(p):
-                rcopy(self.src(p), self.dst.at[p], self.ss.at[p], self.rs.at[p], self.at(p)).wait_send()
-            self.each(go)
+            self.all().wait_send()
 
     def one(buf):
         return lambda p: buf.at[0]
@@ -275,15 +276,12 @@
     def local(src, dst, sem):
         return pltpu.make_async_copy(src, dst, sem)
 
-    def l_own(s):
-        return local(lr.at[s], w.lfull.at[s, pl.ds(shard_rows(t), Q), :], w.l_lr.at[s])
-
-    def loads(s):
-        return (
-            local(rr.at[s], w.rv.at[s], w.l_rv.at[s]),
-            local(lf.at[s], w.lfv.at[s], w.l_lf.at[s]),
-            local(rf.at[s], w.rfv.at[s], w.l_rf.at[s]),
-        )
+    loads = {
+        "lr": local(lr, w.lfull.at[:, pl.ds(shard_rows(t), Q), :], w.l_lr.at[0]),
+        "rv": local(rr, w.rv, w.l_rv.at[0]),
+        "lf": local(lf, w.lfv, w.l_lf.at[0]),
+        "rf": local(rf, w.rfv, w.l_rf.at[0]),
+    }
 
     inputs[0].wait()
     spread = hot(imod(iota((c.NBC, NB), 1), c.NBC) == iota((c.NBC, NB), 0))
@@ -342,10 +340,8 @@
     xB.start()
     w.rA[pl.ds(me_z, 1)] = w.sA[pl.ds(me_z, 1)]
     w.zb[pl.ds(me_g, 1), pl.ds(t, 1), pl.ds(me_z, 1)] = w.sB[pl.ds(me_z, 1)][None, None]
-    for s in range(CAP):
-        l_own(s).start()
-        for copy in loads(s):
-            copy.start()
+    for copy in loads.values():
+        copy.start()
 
     inputs[2].wait()
     adam_col = jnp.zeros((NB, 1), F32)
@@ -442,11 +438,11 @@
     b_core(1).start()
     b_core(c.NY - 1).start()
 
+    loads["lr"].wait()
+    loads["rv"].wait()
     norm_row = jnp.zeros((1, LANES), F32)
 
     def precond(s, dest, at):
-        l_own(s).wait()
-        local(rr.at[s], w.rv.at[s], w.l_rv.at[s]).wait()
         for d in (0, 1):
             l_pass(s, d).wait_recv()
             if s < MAIN:
@@ -507,17 +503,16 @@
     w.ax[...] = jnp.sum(w.agr[...], axis=0, keepdims=True)
     xx.start()
     w.axr[pl.ds(t, 1)] = w.ax[...]
+    loads["lf"].wait()
+    loads["rf"].wait()
+
     def factor(s):
-        local(lf.at[s], w.lfv.at[s], w.l_lf.at[s]).wait()
-        local(rf.at[s], w.rfv.at[s], w.l_rf.at[s]).wait()
         rows = w.gfull[s, pl.ds(shard_rows(t), Q), :]
         gram = lax.dot_general(rows, w.gfull[s], (((1,), (1,)), ((), ())), preferred_element_type=F32)
         w.lnv[s] = (0.9 * w.lfv[s].astype(F32) + 0.1 * gram).astype(BF)
-        local(w.lnv.at[s], ln.at[s], w.l_ln.at[s]).start()
         cols = w.gfull[s, :, pl.ds(shard_rows(t), Q)]
         gram = lax.dot_general(cols, w.gfull[s], (((0,), (0,)), ((), ())), preferred_element_type=F32)
         w.rnv[s] = (0.9 * w.rfv[s].astype(F32) + 0.1 * gram).astype(BF)
-        local(w.rnv.at[s], rn.at[s], w.l_rn.at[s]).start()
 
     for s in range(MAIN):
         factor(s)
@@ -536,12 +531,13 @@
     xwg.start()
     w.wgr[pl.ds(me_g, 1)] = w.wg[...]
 
+    hits = (held_col == slot_row) & (mz == bz_)
+    sel_rest = [hot(hits & (mr == r)) for r in range(R)]
     xH.recv()
     flat = [w.rH[:, :, :, r * Q:(r + 1) * Q].reshape(PS, Q) for r in range(R)]
-    hits = (held_col == slot_row) & (mz == bz_)
     total = jnp.zeros((PB, Q), F32)
     for r in range(R):
-        total += dot(hot(hits & (mr == r)), flat[r])
+        total += dot(sel_rest[r], flat[r])
     w.sJ[...] = total.astype(BF).reshape(NZ, R * CB, Q)
     xJ.start()
     w.rJ[pl.ds(me_z, 1)] = w.sJ[pl.ds(me_z, 1)]
@@ -553,8 +549,12 @@
 
     for s in range(MAIN, CAP):
         factor(s)
+    factors = (local(w.lnv, ln, w.l_ln.at[0]), local(w.rnv, rn, w.l_rn.at[0]))
+    for copy in factors:
+        copy.start()
 
     sel_back = hot(key_col == key_main(iota((1, places), 1)))
+    rest_back = [hot(rest_col == jnp.where(lrr == r, l_rest, -2)) for r in range(R)]
     xI.recv()
     main_part = [dot(sel_back, w.rI[:, :, r * Q:(r + 1) * Q].reshape(places, Q)) for r in range(R)]
     xwz.recv()
@@ -567,7 +567,7 @@
     xJ.recv()
     rest = w.rJ[...].reshape(PB, Q)
     for r in range(R):
-        out = main_part[r] + dot(hot(rest_col == jnp.where(lrr == r, l_rest, -2)), rest)
+        out = main_part[r] + dot(rest_back[r], rest)
         upd[:, r, :, :] = (out * scale_col).astype(BF).reshape(c.NBR, c.NBC, Q)
 
     outputs[1].start()
@@ -586,9 +586,8 @@
             g_pass(s, d).wait_send()
     for k in range(c.NY):
         b_core(k).wait_send()
-    for s in range(CAP):
-        local(w.lnv.at[s], ln.at[s], w.l_ln.at[s]).wait()
-        local(w.rnv.at[s], rn.at[s], w.l_rn.at[s]).wait()
+    for copy in factors:
+        copy.wait()
 
 
 def finish(results):

time: 90.8 us -> 86.7 us (0.955)
  Pallas kernels: 88.7 us -> 84.7 us
    pallas_call x1, Pallas kernels: 86.4 us -> 82.3 us  [step(): pl.pallas_call(functools.partial(kernel, c, tuple(scratch)), out_shape=(l...]
where the time goes in v3:
time: 86.7 us; the launch traced here: 86.5 us
  Pallas kernels  84.7 us (98%)
  between operations  1.53 us (2%)
    pallas_call x1, Pallas kernels, step(): pl.pallas_call(functools.partial(kernel, c, tuple(scratch)), out_shape=(l...  82.3 us
    pallas_call x1, Pallas kernels, finish(): pl.pallas_call(body, out_shape=tuple((jax.ShapeDtypeStruct(a.shape, a.dty...  2.37 us

profile of v3, /device:TPU:1, one launch (start us, length us, event | category | flops | bytes accessed | tf_op | source)
XLA Modules:
  0.0 86.5 jit_solution(13157637662694800358)
XLA Ops:
  0.6 0.0 copy-start
  0.6 0.0 copy-start.1
  0.7 0.0 copy-start.2
  0.7 82.3 %shampoo.3 = (bf16[16,4,16,128]{3,2,1,0:T(8,128)(2,1)}, bf16[16,4,16,128]{3,2,1,0:T(8,128)(2,1)}, bf16[5,128,512]{2,1,0:T(8,128)(2,1)}, bf16[5,128,512]{2,1,0:T(8,128)(2,1)}, s32[1]{0:T(128)}) custom-call(bf16[16,4,16,128]{3,2,1,0:T(8,128)(2,1)} %grads_in.1, bf16[16,4,16,128]{3,2,1,0:T(8,128)(2,1)} %sm_in.1, s32[16,16]{1,0:T(8,128)} %owner_in.1, ...), custom_call_target="tpu_custom_call" | custom-call | tf_op jit(solution)/shard_map/shampoo/pallas_call | solution.py:623
  83.0 0.0 copy-start.3
  83.7 0.0 copy-done
  83.7 0.0 copy-done.1
  83.7 0.0 copy-done.2
  83.7 0.0 copy-done.3
  83.7 2.6 %conditional.1 = ((bf16[16,4,16,128]{3,2,1,0:T(8,128)(2,1)}, bf16[16,4,16,128]{3,2,1,0:T(8,128)(2,1)}, bf16[5,128,512]{2,1,0:T(8,128)(2,1)}, bf16[5,128,512]{2,1,0:T(8,128)(2,1)})) conditional(s32[]{:T(128)} %bitcast, (bf16[16,4,16,128]{3,2,1,0:T(8,128)(2,1)}, bf16[16,4,16,128]{3,2,1,0:T(8,128)(2,1)}, s32[16,16]{1,0:T(8,128)S(1)}, ...), branch_computations={%region_0.0_spmd, %region_1.0_spmd} | conditional | bytes 8 | solution.py:641
  83.9 2.4 %finish.3 = (bf16[16,4,16,128]{3,2,1,0:T(8,128)(2,1)}, bf16[16,4,16,128]{3,2,1,0:T(8,128)(2,1)}, bf16[5,128,512]{2,1,0:T(8,128)(2,1)}, bf16[5,128,512]{2,1,0:T(8,128)(2,1)}) custom-call(bf16[16,4,16,128]{3,2,1,0:T(8,128)(2,1)} %get-tuple-element.33.refs_0_, bf16[16,4,16,128]{3,2,1,0:T(8,128)(2,1)} %get-tuple-element.34.refs_1_, ...), custom_call_target="tpu_custom_call" | custom-call | tf_op jit(solution)/shard_map/cond/branch_1_fun/finish/pallas_call | solution.py:607
Async XLA Ops:
  0.6 83.0 %copy-start = (bf16[5,128,512]{2,1,0:T(8,128)(2,1)S(1)}, bf16[5,128,512]{2,1,0:T(8,128)(2,1)}, u32[]{:S(2)}) copy-start(bf16[5,128,512]{2,1,0:T(8,128)(2,1)} %lf.1) | copy-start | bytes 1966084
  0.6 83.0 %copy-start.1 = (bf16[5,128,512]{2,1,0:T(8,128)(2,1)S(1)}, bf16[5,128,512]{2,1,0:T(8,128)(2,1)}, u32[]{:S(2)}) copy-start(bf16[5,128,512]{2,1,0:T(8,128)(2,1)} %rf.1) | copy-start | bytes 1966084
  0.7 83.0 %copy-start.2 = (bf16[5,128,512]{2,1,0:T(8,128)(2,1)S(1)}, bf16[5,128,512]{2,1,0:T(8,128)(2,1)}, u32[]{:S(2)}) copy-start(bf16[5,128,512]{2,1,0:T(8,128)(2,1)} %lr.1) | copy-start | bytes 1966084
  83.0 0.7 copy-start.3
